TPU v7x, 32 devices: a whole 2x2x4 slice. The times are simulated.
32 devices in a mesh: dp: 8 (over z, x), mp: 4 (over y, core).
Axes of the slice: x: 2, y: 2, z: 4, core: 2. Of those that a mesh axis runs over, the one named last changes fastest.
Arguments:
- tokens: bfloat16 [16384, 2048], P('dp'), may hold values from -0.75 to 0.75
- out_grad: bfloat16 [16384, 2048], P('dp'), may hold values from -3 to 3
- down_rows: bfloat16 [2048, 2048], P(('dp', 'mp')), may hold values from -1 to 1
- up_rows: bfloat16 [2048, 2048], P(('dp', 'mp')), may hold values from -1 to 1
- requests: int32 [32, 32, 2], P(('dp', 'mp')), may hold values from 0 to 64, as said below
- places: int32 [8, 16384, 16], P('mp', 'dp'), may hold values from 0 to 63, as said below
- gate_weights: float32 [8, 16384, 16], P('mp', 'dp'), may hold values from 0.05 to 0.5
Outputs:
- input_grad: bfloat16 [16384, 2048], P(('dp', 'mp'))
- down_grad: float32 [2048, 2048], P(('dp', 'mp'))
- up_grad: float32 [2048, 2048], P(('dp', 'mp'))
Inputs may be any that keep to these rules, and one draw needn't show every extreme that they name: requests[d, o] lists distinct rows, numbered within owner o's block of 64, that device d uses; the used ones come first and the rest of the 2 places hold 64. Every device uses at least one row of every owner, and all 2 places of some owner. The 16 entries of one head and token are distinct places, each of which names an expert in the request list of the device holding that head and token.
All inputs are finite; a program needn't handle non-finite values.
Results may differ from a plain program's by a relative error of at most 0.013.
Values may be sent and summed in bfloat16 or wider, within the bound.
A program may use at most 128 MiB of HBM per device.

v0:
```python
import jax
import jax.numpy as jnp
from jax import lax
from jax.sharding import PartitionSpec as P

SQRT_HALF = 0.7071067811865476
INV_ROOT_TAU = 0.3989422804014327


def gelu_parts(pre):
    normal_cdf = 0.5 * (1.0 + lax.erf(pre * SQRT_HALF))
    density = INV_ROOT_TAU * jnp.exp(-0.5 * pre * pre)
    return (pre * normal_cdf, normal_cdf + pre * density)


def local_terms(block_tokens, block_grad, fetched_down, fetched_up, block_places, block_gates):
    token_count = block_tokens.shape[0]
    place_count = fetched_down.shape[0]
    chosen = jnp.transpose(block_places, (1, 0, 2)).reshape(token_count, -1)
    weights_in = jnp.transpose(block_gates, (1, 0, 2)).reshape(token_count, -1)
    columns = jnp.arange(place_count, dtype=jnp.int32)
    weight = jnp.sum(
        jnp.where(
            chosen[:, :, None] == columns[None, None, :],
            weights_in[:, :, None],
            jnp.zeros((), weights_in.dtype),
        ),
        axis=1,
    )
    pre = lax.dot_general(
        block_tokens, fetched_down, (((1,), (1,)), ((), ())), preferred_element_type=jnp.float32
    )
    back = lax.dot_general(
        block_grad, fetched_up, (((1,), (1,)), ((), ())), preferred_element_type=jnp.float32
    )
    active, slope = gelu_parts(pre)
    coef = (weight * slope * back).astype(jnp.bfloat16)
    gated = (weight * active).astype(jnp.bfloat16)
    part_down = lax.dot_general(
        coef, block_tokens, (((0,), (0,)), ((), ())), preferred_element_type=jnp.float32
    )
    part_up = lax.dot_general(
        gated, block_grad, (((0,), (0,)), ((), ())), preferred_element_type=jnp.float32
    )
    return (coef, part_down, part_up)


def shards(tokens, out_grad, down_rows, up_rows, requests, places, gate_weights):
    n_data = lax.axis_size("dp")
    n_model = lax.axis_size("mp")
    devices = n_data * n_model
    row_count = down_rows.shape[0]
    width = tokens.shape[1]
    wanted = requests[0]
    capacity = wanted.shape[1]
    asked = lax.all_to_all(wanted, ("dp", "mp"), split_axis=0, concat_axis=0, tiled=True)
    live = (wanted < row_count).reshape(-1)
    table = jnp.concatenate([down_rows, up_rows], axis=1)
    outgoing = jnp.take(table, jnp.minimum(asked, row_count - 1).reshape(-1), axis=0).reshape(
        devices, capacity, 2 * width
    )
    arrived = lax.all_to_all(outgoing, ("dp", "mp"), split_axis=0, concat_axis=0, tiled=True)
    arrived = arrived.reshape(devices * capacity, 2 * width)
    arrived = jnp.where(live[:, None], arrived, jnp.zeros((), arrived.dtype))
    fetched_down = arrived[:, :width]
    fetched_up = arrived[:, width:]
    coef, part_down, part_up = local_terms(
        tokens, out_grad, fetched_down, fetched_up, places, gate_weights
    )
    pushed = jnp.concatenate([part_down, part_up], axis=1).reshape(devices, capacity, 2 * width)
    returned = lax.all_to_all(
        pushed.astype(jnp.bfloat16), ("dp", "mp"), split_axis=0, concat_axis=0, tiled=True
    ).astype(pushed.dtype)
    returned = returned.reshape(devices * capacity, 2 * width)
    selector = (asked.reshape(1, -1) == jnp.arange(row_count, dtype=jnp.int32)[:, None]).astype(
        jnp.float32
    )
    summed = jnp.dot(
        selector, returned, precision=lax.Precision.HIGHEST, preferred_element_type=jnp.float32
    )
    down_grad = summed[:, :width]
    up_grad = summed[:, width:]
    input_grad = lax.psum_scatter(
        jnp.dot(coef, fetched_down, preferred_element_type=jnp.float32).astype(jnp.bfloat16),
        "mp",
        scatter_dimension=0,
        tiled=True,
    )
    return (input_grad, down_grad, up_grad)


def solution(mesh):
    in_specs = (
        P("dp", None),
        P("dp", None),
        P(("dp", "mp"), None),
        P(("dp", "mp"), None),
        P(("dp", "mp"), None, None),
        P("mp", "dp", None),
        P("mp", "dp", None),
    )
    out_specs = (P(("dp", "mp"), None), P(("dp", "mp"), None), P(("dp", "mp"), None))
    return jax.shard_map(shards, mesh=mesh, in_specs=in_specs, out_specs=out_specs, check_vma=False)
```

profile of v0, /device:TPU:0, one launch (start us, length us, event | category | flops | bytes accessed | tf_op | source)
XLA Modules:
  0.0 142.1 jit_solution(13658119009463348901)
XLA Ops:
  7.2 0.0 copy-start.2
  7.2 0.0 copy-start
  7.2 0.0 copy-start.1
  7.2 1.4 %copy.29 = s32[32,1,2]{2,1,0:T(1,128)} copy(s32[32,1,2]{0,2,1:T(2,128)} %bitcast.28) | data formatting | bytes 512 | tf_op jit(solution)/shard_map/all_to_all | solution.py:56
  8.6 7.3 %all-to-all-start = ((s32[32,1,2]{2,1,0:T(1,128)}), s32[32,1,2]{2,1,0:T(1,128)S(1)}, u32[]{:S(2)}, u32[]{:S(2)}) async-start(s32[32,1,2]{2,1,0:T(1,128)} %copy.29), calls=%async_computation | async-start | bytes 32768 | tf_op jit(solution)/shard_map/all_to_all | solution.py:56
  15.9 1.1 pad_maximum_fusion
  17.0 6.0 %all-to-all-done = s32[32,1,2]{2,1,0:T(1,128)S(1)} async-done(((s32[32,1,2]{2,1,0:T(1,128)}), s32[32,1,2]{2,1,0:T(1,128)S(1)}, u32[]{:S(2)}, u32[]{:S(2)}) %all-to-all-start) | async-done | bytes 288 | tf_op jit(solution)/shard_map/all_to_all | solution.py:56
  23.0 0.5 broadcast.62
  23.5 0.7 fusion.14
  24.2 0.1 min.29
  24.4 0.1 copy.30
  24.5 0.1 copy.31
  24.6 0.9 gather_fusion
  25.4 0.3 gather.7
  25.8 1.4 broadcast_select_fusion
  27.1 2.6 %all-to-all-start.1 = ((bf16[32,2,4096]{2,1,0:T(2,128)(2,1)}), bf16[32,2,4096]{2,1,0:T(2,128)(2,1)S(1)}, u32[]{:S(2)}, u32[]{:S(2)}) async-start(bf16[32,2,4096]{2,1,0:T(2,128)(2,1)} %broadcast_select_fusion), calls=%async_computation.1 | async-start | bytes 1048576 | tf_op jit(solution)/shard_map/all_to_all | solution.py:62
  29.8 0.0 reduce-scatter.2.cloned.1.call-start
  29.8 0.0 copy-done.2
  29.8 0.1 copy.28
  29.9 0.1 lt.39
  30.0 0.0 copy-done
  30.1 0.0 copy-done.1
  30.1 3.1 %select_reduce_fusion = f32[2048,64]{0,1:T(8,128)S(1)} fusion(f32[2048,32]{0,1:T(8,128)S(1)} %bitcast.26, s32[2048,32]{0,1:T(8,128)S(1)} %bitcast.27), kind=kLoop, calls=%fused_computation.1 | loop fusion | flops 12451840 | bytes 1048576 | tf_op jit(solution)/shard_map/reduce_sum | solution.py:22
  33.1 12.2 %all-to-all-done.1 = bf16[32,2,4096]{2,1,0:T(2,128)(2,1)S(1)} async-done(((bf16[32,2,4096]{2,1,0:T(2,128)(2,1)}), bf16[32,2,4096]{2,1,0:T(2,128)(2,1)S(1)}, u32[]{:S(2)}, u32[]{:S(2)}) %all-to-all-start.1) | async-done | bytes 524320 | tf_op jit(solution)/shard_map/all_to_all | solution.py:62
  45.3 0.2 reshape.67
  45.5 0.1 broadcast_select_fusion.1
  45.6 6.0 %convolution_bitcast_fusion.1 = f32[2048,64]{0,1:T(8,128)S(1)} fusion(bf16[2048,2048]{1,0:T(8,128)(2,1)} %param.7, bf16[64,4096]{1,0:T(8,128)(2,1)S(1)} %broadcast_select_fusion.1), kind=kOutput, calls=%fused_computation.6 | convolution fusion | flops 536870912 | bytes 9175040 | tf_op jit(solution)/shard_map/dot_general | solution.py:30
  51.7 6.1 %fusion.1 = bf16[2048,64]{0,1:T(8,128)(2,1)S(1)} fusion(bf16[2048,2048]{1,0:T(8,128)(2,1)} %param.8, f32[2048,64]{0,1:T(8,128)S(1)} %select_reduce_fusion, f32[2048,64]{0,1:T(8,128)S(1)} %convolution_bitcast_fusion.1, bf16[64,4096]{1,0:T(8,128)(2,1)S(1)} %broadcast_select_fusion.1), kind=kOutput, calls=%fused_computation.7 | convolution fusion | flops 538312704 | bytes 9961472 | tf_op jit(solution)/shard_map/dot_general | solution.py:33
  57.7 5.6 %convolution_convert_fusion = bf16[2048,2048]{1,0:T(8,128)(2,1)} fusion(bf16[2048,64]{0,1:T(8,128)(2,1)S(1)} %fusion.1, bf16[64,4096]{1,0:T(8,128)(2,1)S(1)} %broadcast_select_fusion.1), kind=kOutput, calls=%fused_computation.3 | convolution fusion | flops 541065216 | bytes 8912896 | tf_op jit(solution)/shard_map/dot_general | solution.py:84
  63.3 0.0 reduce-scatter.2.cloned.1.call-update
  63.4 5.0 %convolution_convert_fusion.2 = bf16[64,2048]{1,0:T(8,128)(2,1)S(1)} fusion(bf16[2048,64]{0,1:T(8,128)(2,1)S(1)} %fusion.1, bf16[2048,2048]{1,0:T(8,128)(2,1)} %param.7), kind=kOutput, calls=%fused_computation.9 | convolution fusion | flops 537001984 | bytes 8912896 | tf_op jit(solution)/shard_map/dot_general | solution.py:39
  68.3 6.6 %convolution_convert_fusion.1 = bf16[64,2048]{1,0:T(8,128)(2,1)S(1)} fusion(bf16[2048,2048]{1,0:T(8,128)(2,1)} %param.8, f32[2048,64]{0,1:T(8,128)S(1)} %select_reduce_fusion, f32[2048,64]{0,1:T(8,128)S(1)} %convolution_bitcast_fusion.1), kind=kOutput, calls=%fused_computation.8 | convolution fusion | flops 537788416 | bytes 9699328 | tf_op jit(solution)/shard_map/dot_general | solution.py:42
  75.0 1.1 convert_element_type.18
  76.1 2.6 %all-to-all-start.2 = ((bf16[32,2,4096]{2,1,0:T(2,128)(2,1)}), bf16[32,2,4096]{2,1,0:T(2,128)(2,1)S(1)}, u32[]{:S(2)}, u32[]{:S(2)}) async-start(bf16[32,2,4096]{2,1,0:T(2,128)(2,1)} %convert_element_type.18), calls=%async_computation.3 | async-start | bytes 1048576 | tf_op jit(solution)/shard_map/all_to_all | solution.py:71
  78.7 0.1 all_to_all.17
  78.8 15.4 %all-to-all-done.2 = bf16[32,2,4096]{2,1,0:T(2,128)(2,1)S(1)} async-done(((bf16[32,2,4096]{2,1,0:T(2,128)(2,1)}), bf16[32,2,4096]{2,1,0:T(2,128)(2,1)S(1)}, u32[]{:S(2)}, u32[]{:S(2)}) %all-to-all-start.2) | async-done | bytes 524320 | tf_op jit(solution)/shard_map/all_to_all | solution.py:71
  94.3 0.2 reshape.68
  94.5 0.3 fusion.10
  94.8 1.1 fusion.15
  95.8 39.4 %reduce-scatter.2.cloned.1.call-done = bf16[512,2048]{1,0:T(8,128)(2,1)} async-done(((bf16[2048,2048]{1,0:T(8,128)(2,1)}), bf16[512,2048]{1,0:T(8,128)(2,1)}) %reduce-scatter.2.cloned.1.call-update) | async-done | bytes 2097168 | tf_op jit(solution)/shard_map/reduce_scatter | solution.py:83
  (5 shorter events, 0.1 us)
Async XLA Ops:
  7.2 22.6 %copy-start.2 = (s32[1,32,2]{1,2,0:T(2,128)S(1)}, s32[1,32,2]{1,2,0:T(2,128)}, u32[]{:S(2)}) copy-start(s32[1,32,2]{1,2,0:T(2,128)} %param.11) | copy-start | bytes 772
  7.2 22.9 %copy-start = (f32[2,2048,16]{1,2,0:T(8,128)S(1)}, f32[2,2048,16]{1,2,0:T(8,128)}, u32[]{:S(2)}) copy-start(f32[2,2048,16]{1,2,0:T(8,128)} %param.13) | copy-start | bytes 786436
  7.2 22.9 %copy-start.1 = (s32[2,2048,16]{1,2,0:T(8,128)S(1)}, s32[2,2048,16]{1,2,0:T(8,128)}, u32[]{:S(2)}) copy-start(s32[2,2048,16]{1,2,0:T(8,128)} %param.12) | copy-start | bytes 786436
  8.6 14.4 %all-to-all-start = ((s32[32,1,2]{2,1,0:T(1,128)}), s32[32,1,2]{2,1,0:T(1,128)S(1)}, u32[]{:S(2)}, u32[]{:S(2)}) async-start(s32[32,1,2]{2,1,0:T(1,128)} %copy.29), calls=%async_computation | async-start | bytes 32768 | tf_op jit(solution)/shard_map/all_to_all | solution.py:56
  27.1 18.2 %all-to-all-start.1 = ((bf16[32,2,4096]{2,1,0:T(2,128)(2,1)}), bf16[32,2,4096]{2,1,0:T(2,128)(2,1)S(1)}, u32[]{:S(2)}, u32[]{:S(2)}) async-start(bf16[32,2,4096]{2,1,0:T(2,128)(2,1)} %broadcast_select_fusion), calls=%async_computation.1 | async-start | bytes 1048576 | tf_op jit(solution)/shard_map/all_to_all | solution.py:62
  29.8 105.5 %reduce-scatter.2.cloned.1.call-start = ((), (), s32[]{:S(2)}) async-start(), calls=%async_computation.4 | async-start | bytes 10485760 | tf_op jit(solution)/shard_map/reduce_scatter | solution.py:83
  76.1 18.2 %all-to-all-start.2 = ((bf16[32,2,4096]{2,1,0:T(2,128)(2,1)}), bf16[32,2,4096]{2,1,0:T(2,128)(2,1)S(1)}, u32[]{:S(2)}, u32[]{:S(2)}) async-start(bf16[32,2,4096]{2,1,0:T(2,128)(2,1)} %convert_element_type.18), calls=%async_computation.3 | async-start | bytes 1048576 | tf_op jit(solution)/shard_map/all_to_all | solution.py:71
Sparse Core Ops, SparseCore 0:
  63.5 71.7 reduce-scatter.1
where the time goes:
time: 143 us; the launch traced here: 142 us
  waiting for transfers between devices  73 us (51%)
  matrix products  29.6 us (21%)
  between operations  14.2 us (10%)
  starting transfers between devices  12.6 us (9%)
  other arithmetic  6.39 us (4%)
  local copies, waits for them, and re-layouts  6.35 us (4%)
    reduce_scatter x1, waiting for transfers between devices, shards(): lax.psum_scatter(jnp.dot(coef, fetched_down, preferred_element_type=jnp.f...  39.4 us
    all_to_all x1, waiting for transfers between devices, shards(): lax.all_to_all(pushed.astype(jnp.bfloat16), ('dp', 'mp'), split_axis=0, c...  15.4 us
    all_to_all x1, waiting for transfers between devices, shards(): lax.all_to_all(outgoing, ('dp', 'mp'), split_axis=0, concat_axis=0, tiled...  12.2 us
    all_to_all x1, starting transfers between devices, shards(): lax.all_to_all(wanted, ('dp', 'mp'), split_axis=0, concat_axis=0, tiled=T...  7.3 us
    dot_general x1, matrix products, local_terms(): lax.dot_general(gated, block_grad, (((0,), (0,)), ((), ())), preferred_el...  6.61 us
    dot_general x1, matrix products, local_terms(): lax.dot_general(block_grad, fetched_up, (((1,), (1,)), ((), ())), preferr...  6.07 us
    dot_general x1, matrix products, local_terms(): lax.dot_general(block_tokens, fetched_down, (((1,), (1,)), ((), ())), pre...  6.04 us
    all_to_all x1, waiting for transfers between devices, shards(): lax.all_to_all(wanted, ('dp', 'mp'), split_axis=0, concat_axis=0, tiled=T...  6 us
  transfers between devices with their start and end apart: 4, of which 4 were waited for; matrix products, arithmetic and copies ran while one was open for 13% of the time, Pallas kernels for 0%

commit v1 on v0

--- a/solution.py
+++ b/solution.py
@@ -67,6 +67,12 @@
     coef, part_down, part_up = local_terms(
         tokens, out_grad, fetched_down, fetched_up, places, gate_weights
     )
+    token_count = tokens.shape[0] // n_model
+    group_down = lax.all_gather(fetched_down, "mp", axis=0, tiled=True)
+    mine = lax.all_to_all(
+        coef.reshape(n_model, token_count, -1), "mp", split_axis=0, concat_axis=0, tiled=True
+    )
+    mine = jnp.transpose(mine, (1, 0, 2)).reshape(token_count, -1)
     pushed = jnp.concatenate([part_down, part_up], axis=1).reshape(devices, capacity, 2 * width)
     returned = lax.all_to_all(
         pushed.astype(jnp.bfloat16), ("dp", "mp"), split_axis=0, concat_axis=0, tiled=True
@@ -80,12 +86,9 @@
     )
     down_grad = summed[:, :width]
     up_grad = summed[:, width:]
-    input_grad = lax.psum_scatter(
-        jnp.dot(coef, fetched_down, preferred_element_type=jnp.float32).astype(jnp.bfloat16),
-        "mp",
-        scatter_dimension=0,
-        tiled=True,
-    )
+    input_grad = jnp.dot(
+        mine, group_down, preferred_element_type=jnp.float32
+    ).astype(jnp.bfloat16)
     return (input_grad, down_grad, up_grad)
 
 

time: 143 us -> 102 us (0.71)
  waiting for transfers between devices: 73 us -> 36.6 us
  matrix products: 29.6 us -> 19.1 us
  starting transfers between devices: 12.6 us -> 16.3 us
  local copies, waits for them, and re-layouts: 6.35 us -> 8.41 us
    reduce_scatter x1 -> x0, waiting for transfers between devices: 39.4 us -> none  [shards(): lax.psum_scatter(jnp.dot(coef, fetched_down, preferred_element_type=jnp.f...]
    dot_general x1, matrix products: 6.61 us -> 1.58 us  [local_terms(): lax.dot_general(gated, block_grad, (((0,), (0,)), ((), ())), preferred_el...]
    all_to_all x0 -> x1, waiting for transfers between devices: none -> 4.43 us  [shards(): lax.all_to_all(coef.reshape(n_model, token_count, -1), 'mp', split_axis=0...]
    all_to_all x0 -> x1, starting transfers between devices: none -> 3.41 us  [shards(): lax.all_to_all(coef.reshape(n_model, token_count, -1), 'mp', split_axis=0...]
    dot_general x1, matrix products: 4.95 us -> 1.59 us  [local_terms(): lax.dot_general(coef, block_tokens, (((0,), (0,)), ((), ())), preferred_e...]
    dot_general x1, matrix products: 5.6 us -> 3.28 us  [shards(): jnp.dot(mine, group_down, preferred_element_type=jnp.float32)]
    all_to_all x1, waiting for transfers between devices: 15.4 us -> 13.9 us  [shards(): lax.all_to_all(pushed.astype(jnp.bfloat16), ('dp', 'mp'), split_axis=0, c...]
  transfers between devices with their start and end apart: 4 -> 5, of which waited for: 4 -> 4; matrix products, arithmetic and copies ran while one was open for 13% -> 7% of each run, Pallas kernels for 0% -> 0%
where the time goes in v1:
time: 102 us; the launch traced here: 101 us
  waiting for transfers between devices  36.6 us (36%)
  matrix products  19.1 us (19%)
  starting transfers between devices  16.3 us (16%)
  between operations  14.3 us (14%)
  local copies, waits for them, and re-layouts  8.41 us (8%)
  other arithmetic  6.38 us (6%)
    all_to_all x1, waiting for transfers between devices, shards(): lax.all_to_all(pushed.astype(jnp.bfloat16), ('dp', 'mp'), split_axis=0, c...  13.9 us
    all_to_all x1, waiting for transfers between devices, shards(): lax.all_to_all(outgoing, ('dp', 'mp'), split_axis=0, concat_axis=0, tiled...  12.2 us
    all_to_all x1, starting transfers between devices, shards(): lax.all_to_all(wanted, ('dp', 'mp'), split_axis=0, concat_axis=0, tiled=T...  7.3 us
    dot_general x1, matrix products, local_terms(): lax.dot_general(block_grad, fetched_up, (((1,), (1,)), ((), ())), preferr...  6.21 us
    dot_general x1, matrix products, local_terms(): lax.dot_general(block_tokens, fetched_down, (((1,), (1,)), ((), ())), pre...  6.19 us
    all_to_all x1, waiting for transfers between devices, shards(): lax.all_to_all(wanted, ('dp', 'mp'), split_axis=0, concat_axis=0, tiled=T...  6 us
    all_to_all x1, waiting for transfers between devices, shards(): lax.all_to_all(coef.reshape(n_model, token_count, -1), 'mp', split_axis=0...  4.43 us
    all_to_all x1, starting transfers between devices, shards(): lax.all_to_all(coef.reshape(n_model, token_count, -1), 'mp', split_axis=0...  3.41 us
  transfers between devices with their start and end apart: 5, of which 4 were waited for; matrix products, arithmetic and copies ran while one was open for 7% of the time, Pallas kernels for 0%

profile of v1, /device:TPU:0, one launch (start us, length us, event | category | flops | bytes accessed | tf_op | source)
XLA Modules:
  0.0 101.1 jit_solution(4183324993623743926)
XLA Ops:
  7.2 0.0 copy-start.2
  7.2 0.0 copy-start
  7.2 0.0 copy-start.1
  7.2 1.4 %copy.31 = s32[32,1,2]{2,1,0:T(1,128)} copy(s32[32,1,2]{0,2,1:T(2,128)} %bitcast.42) | data formatting | bytes 512 | tf_op jit(solution)/shard_map/all_to_all | solution.py:56
  8.6 7.3 %all-to-all-start = ((s32[32,1,2]{2,1,0:T(1,128)}), s32[32,1,2]{2,1,0:T(1,128)S(1)}, u32[]{:S(2)}, u32[]{:S(2)}) async-start(s32[32,1,2]{2,1,0:T(1,128)} %copy.31), calls=%async_computation | async-start | bytes 32768 | tf_op jit(solution)/shard_map/all_to_all | solution.py:56
  15.9 1.1 %pad_maximum_fusion = bf16[64,4096]{1,0:T(8,128)(2,1)S(1)} fusion(bf16[64,2048]{1,0:T(8,128)(2,1)} %param.10, bf16[64,2048]{1,0:T(8,128)(2,1)} %param.9), kind=kLoop, calls=%fused_computation.17 | loop fusion | flops 1048576 | bytes 1048576 | tf_op jit(solution)/shard_map/concatenate | solution.py:58
  17.0 6.0 %all-to-all-done = s32[32,1,2]{2,1,0:T(1,128)S(1)} async-done(((s32[32,1,2]{2,1,0:T(1,128)}), s32[32,1,2]{2,1,0:T(1,128)S(1)}, u32[]{:S(2)}, u32[]{:S(2)}) %all-to-all-start) | async-done | bytes 288 | tf_op jit(solution)/shard_map/all_to_all | solution.py:56
  23.0 0.5 broadcast.62
  23.5 0.7 fusion.13
  24.2 0.1 min.29
  24.4 0.1 copy.32
  24.5 0.1 copy.33
  24.6 0.9 gather_fusion
  25.4 0.3 gather.7
  25.8 1.4 %broadcast_select_fusion = bf16[32,2,4096]{2,1,0:T(2,128)(2,1)} fusion(bf16[32,2,4096]{2,1,0:T(2,128)(2,1)S(1)} %gather.7, pred[32,2]{1,0:T(8,128)(4,1)S(1)} %copy.33), kind=kLoop, calls=%fused_computation.10 | loop fusion | flops 262144 | bytes 1048640 | tf_op jit(solution)/shard_map/jit(_take)/select_n | solution.py:59
  27.1 2.6 %all-to-all-start.1 = ((bf16[32,2,4096]{2,1,0:T(2,128)(2,1)}), bf16[32,2,4096]{2,1,0:T(2,128)(2,1)S(1)}, u32[]{:S(2)}, u32[]{:S(2)}) async-start(bf16[32,2,4096]{2,1,0:T(2,128)(2,1)} %broadcast_select_fusion), calls=%async_computation.1 | async-start | bytes 1048576 | tf_op jit(solution)/shard_map/all_to_all | solution.py:62
  29.8 0.1 copy.30
  29.9 0.1 lt.39
  30.0 0.0 copy-done
  30.0 0.0 copy-done.1
  30.0 3.1 %select_reduce_fusion = f32[2048,64]{0,1:T(8,128)S(1)} fusion(f32[2048,32]{0,1:T(8,128)S(1)} %bitcast.40, s32[2048,32]{0,1:T(8,128)S(1)} %bitcast.41), kind=kLoop, calls=%fused_computation.1 | loop fusion | flops 12451840 | bytes 1048576 | tf_op jit(solution)/shard_map/reduce_sum | solution.py:22
  33.1 12.2 %all-to-all-done.1 = bf16[32,2,4096]{2,1,0:T(2,128)(2,1)S(1)} async-done(((bf16[32,2,4096]{2,1,0:T(2,128)(2,1)}), bf16[32,2,4096]{2,1,0:T(2,128)(2,1)S(1)}, u32[]{:S(2)}, u32[]{:S(2)}) %all-to-all-start.1) | async-done | bytes 524320 | tf_op jit(solution)/shard_map/all_to_all | solution.py:62
  45.3 0.2 reshape.73
  45.5 0.1 broadcast_select_fusion.1
  45.6 0.0 slice-start
  45.6 6.2 %convolution_bitcast_fusion.1 = f32[2048,64]{0,1:T(8,128)S(1)} fusion(bf16[2048,2048]{1,0:T(8,128)(2,1)} %param.7, bf16[64,4096]{1,0:T(8,128)(2,1)S(1)} %broadcast_select_fusion.1), kind=kOutput, calls=%fused_computation.6 | convolution fusion | flops 536870912 | bytes 9175040 | tf_op jit(solution)/shard_map/dot_general | solution.py:30
  51.8 0.0 slice-start.1
  51.8 0.0 slice-start.2
  51.8 6.2 %fusion.1 = bf16[2048,64]{0,1:T(8,128)(2,1)S(1)} fusion(bf16[2048,2048]{1,0:T(8,128)(2,1)} %param.8, f32[2048,64]{0,1:T(8,128)S(1)} %select_reduce_fusion, f32[2048,64]{0,1:T(8,128)S(1)} %convolution_bitcast_fusion.1, bf16[64,4096]{1,0:T(8,128)(2,1)S(1)} %broadcast_select_fusion.1), kind=kOutput, calls=%fused_computation.7 | convolution fusion | flops 538312704 | bytes 9961472 | tf_op jit(solution)/shard_map/dot_general | solution.py:33
  58.1 0.0 slice-done.1
  58.1 0.0 slice-start.3
  58.1 1.6 %convolution_convert_fusion.1 = bf16[64,2048]{1,0:T(8,128)(2,1)S(1)} fusion(bf16[2048,2048]{1,0:T(8,128)(2,1)S(1)} %bitcast.35, f32[2048,64]{0,1:T(8,128)S(1)} %select_reduce_fusion, f32[2048,64]{0,1:T(8,128)S(1)} %convolution_bitcast_fusion.1), kind=kOutput, calls=%fused_computation.8 | convolution fusion | flops 537788416 | bytes 9699328 | tf_op jit(solution)/shard_map/dot_general | solution.py:42
  59.7 0.6 slice-done.3
  60.3 1.6 %convolution_convert_fusion.2 = bf16[64,2048]{1,0:T(8,128)(2,1)S(1)} fusion(bf16[2048,64]{0,1:T(8,128)(2,1)S(1)} %fusion.1, bf16[2048,2048]{1,0:T(8,128)(2,1)S(1)} %bitcast.37), kind=kOutput, calls=%fused_computation.9 | convolution fusion | flops 537001984 | bytes 8912896 | tf_op jit(solution)/shard_map/dot_general | solution.py:39
  61.9 1.1 %convert_element_type.18 = bf16[32,2,4096]{2,1,0:T(2,128)(2,1)} reshape(bf16[64,4096]{1,0:T(8,128)(2,1)S(1)} %pad_maximum_fusion.1) | data formatting | bytes 1048576 | tf_op jit(solution)/shard_map/convert_element_type | solution.py:78
  63.1 3.0 %all-to-all-start.3 = ((bf16[32,2,4096]{2,1,0:T(2,128)(2,1)}), bf16[32,2,4096]{2,1,0:T(2,128)(2,1)S(1)}, u32[]{:S(2)}, u32[]{:S(2)}) async-start(bf16[32,2,4096]{2,1,0:T(2,128)(2,1)} %convert_element_type.18), calls=%async_computation.3 | async-start | bytes 1048576 | tf_op jit(solution)/shard_map/all_to_all | solution.py:77
  66.0 0.0 all-gather.2.cloned.1.call-start
  66.1 0.7 slice.18
  66.8 0.0 all-gather.2.cloned.1.call-update
  66.8 0.1 all_to_all.21
  66.9 0.7 copy.37
  67.7 13.9 %all-to-all-done.3 = bf16[32,2,4096]{2,1,0:T(2,128)(2,1)S(1)} async-done(((bf16[32,2,4096]{2,1,0:T(2,128)(2,1)}), bf16[32,2,4096]{2,1,0:T(2,128)(2,1)S(1)}, u32[]{:S(2)}, u32[]{:S(2)}) %all-to-all-start.3) | async-done | bytes 524320 | tf_op jit(solution)/shard_map/all_to_all | solution.py:77
  81.6 3.4 %all-to-all-start.2 = ((bf16[4,512,64]{1,2,0:T(8,128)(2,1)}), bf16[4,512,64]{1,2,0:T(8,128)(2,1)S(1)}, u32[]{:S(2)}, u32[]{:S(2)}) async-start(bf16[4,512,64]{1,2,0:T(8,128)(2,1)} %bitcast.33), calls=%async_computation.2 | async-start | bytes 524288 | tf_op jit(solution)/shard_map/all_to_all | solution.py:72
  85.0 0.2 reshape.76
  85.2 0.3 fusion.8
  85.5 1.1 %fusion.14 = (f32[64,2048]{1,0:T(8,128)}, f32[64,2048]{1,0:T(8,128)}) fusion(f32[64,4096]{1,0:T(8,128)S(1)} %fusion.8), kind=kLoop, calls=%fused_computation.37 | loop fusion | bytes 2097152 | tf_op jit(solution)/shard_map/slice | solution.py:88
  86.6 4.4 %all-to-all-done.2 = bf16[4,512,64]{1,2,0:T(8,128)(2,1)S(1)} async-done(((bf16[4,512,64]{1,2,0:T(8,128)(2,1)}), bf16[4,512,64]{1,2,0:T(8,128)(2,1)S(1)}, u32[]{:S(2)}, u32[]{:S(2)}) %all-to-all-start.2) | async-done | bytes 262176 | tf_op jit(solution)/shard_map/all_to_all | solution.py:72
  91.0 3.3 %convolution_convert_fusion = bf16[512,2048]{1,0:T(8,128)(2,1)} fusion(bf16[512,256]{0,1:T(8,128)(2,1)S(1)} %bitcast.39, bf16[256,2048]{1,0:T(8,128)(2,1)} %all-gather.2.cloned.1.call-done), kind=kOutput, calls=%fused_computation.3 | convolution fusion | flops 537919488 | bytes 3407872 | tf_op jit(solution)/shard_map/dot_general | solution.py:89
  (11 shorter events, 0.1 us)
Async XLA Ops:
  7.2 22.6 %copy-start.2 = (s32[1,32,2]{1,2,0:T(2,128)S(1)}, s32[1,32,2]{1,2,0:T(2,128)}, u32[]{:S(2)}) copy-start(s32[1,32,2]{1,2,0:T(2,128)} %param.11) | copy-start | bytes 772
  7.2 22.8 %copy-start = (f32[2,2048,16]{1,2,0:T(8,128)S(1)}, f32[2,2048,16]{1,2,0:T(8,128)}, u32[]{:S(2)}) copy-start(f32[2,2048,16]{1,2,0:T(8,128)} %param.13) | copy-start | bytes 786436
  7.2 22.8 %copy-start.1 = (s32[2,2048,16]{1,2,0:T(8,128)S(1)}, s32[2,2048,16]{1,2,0:T(8,128)}, u32[]{:S(2)}) copy-start(s32[2,2048,16]{1,2,0:T(8,128)} %param.12) | copy-start | bytes 786436
  8.6 14.4 %all-to-all-start = ((s32[32,1,2]{2,1,0:T(1,128)}), s32[32,1,2]{2,1,0:T(1,128)S(1)}, u32[]{:S(2)}, u32[]{:S(2)}) async-start(s32[32,1,2]{2,1,0:T(1,128)} %copy.31), calls=%async_computation | async-start | bytes 32768 | tf_op jit(solution)/shard_map/all_to_all | solution.py:56
  27.1 18.2 %all-to-all-start.1 = ((bf16[32,2,4096]{2,1,0:T(2,128)(2,1)}), bf16[32,2,4096]{2,1,0:T(2,128)(2,1)S(1)}, u32[]{:S(2)}, u32[]{:S(2)}) async-start(bf16[32,2,4096]{2,1,0:T(2,128)(2,1)} %broadcast_select_fusion), calls=%async_computation.1 | async-start | bytes 1048576 | tf_op jit(solution)/shard_map/all_to_all | solution.py:62
  45.6 12.4 %slice-start = ((s8[8388608]{0:T(1024)(128)(4,1)}), s8[4194304]{0:T(1024)(128)(4,1)S(1)}, s32[]{:S(2)}) async-start(s8[8388608]{0:T(1024)(128)(4,1)} %bitcast.34), calls=%async_computation.5 | async-start | bytes 8388608
  51.8 6.2 %slice-start.1 = ((s8[8388608]{0:T(1024)(128)(4,1)}), s8[4194304]{0:T(1024)(128)(4,1)S(1)}, s32[]{:S(2)}) async-start(s8[8388608]{0:T(1024)(128)(4,1)} %bitcast.34), calls=%async_computation.6 | async-start | bytes 8388608
  51.8 7.9 %slice-start.2 = ((s8[8388608]{0:T(1024)(128)(4,1)}), s8[4194304]{0:T(1024)(128)(4,1)S(1)}, s32[]{:S(2)}) async-start(s8[8388608]{0:T(1024)(128)(4,1)} %bitcast.36), calls=%async_computation.7 | async-start | bytes 8388608
  58.1 2.2 %slice-start.3 = ((s8[8388608]{0:T(1024)(128)(4,1)}), s8[4194304]{0:T(1024)(128)(4,1)S(1)}, s32[]{:S(2)}) async-start(s8[8388608]{0:T(1024)(128)(4,1)} %bitcast.36), calls=%async_computation.8 | async-start | bytes 8388608
  63.1 18.5 %all-to-all-start.3 = ((bf16[32,2,4096]{2,1,0:T(2,128)(2,1)}), bf16[32,2,4096]{2,1,0:T(2,128)(2,1)S(1)}, u32[]{:S(2)}, u32[]{:S(2)}) async-start(bf16[32,2,4096]{2,1,0:T(2,128)(2,1)} %convert_element_type.18), calls=%async_computation.3 | async-start | bytes 1048576 | tf_op jit(solution)/shard_map/all_to_all | solution.py:77
  66.0 25.0 %all-gather.2.cloned.1.call-start = ((), (), s32[]{:S(2)}) async-start(), calls=%async_computation.4 | async-start | bytes 1310720 | tf_op jit(solution)/shard_map/all_gather | solution.py:71
  81.6 9.4 %all-to-all-start.2 = ((bf16[4,512,64]{1,2,0:T(8,128)(2,1)}), bf16[4,512,64]{1,2,0:T(8,128)(2,1)S(1)}, u32[]{:S(2)}, u32[]{:S(2)}) async-start(bf16[4,512,64]{1,2,0:T(8,128)(2,1)} %bitcast.33), calls=%async_computation.2 | async-start | bytes 524288 | tf_op jit(solution)/shard_map/all_to_all | solution.py:72
Sparse Core Ops, SparseCore 0:
  68.4 18.6 all-gather.1

commit v2 on v0

v2 whole, which is shorter than its diff:
```python
import functools

import jax
import jax.numpy as jnp
from jax import lax
from jax.experimental import pallas as pl
from jax.experimental.pallas import tpu as pltpu
from jax.sharding import PartitionSpec as P

SQRT_HALF = 0.7071067811865476
INV_ROOT_TAU = 0.3989422804014327
F32 = jnp.float32
BF16 = jnp.bfloat16
GROUP = 8
MESH = pl.DeviceIdType.MESH


def gelu_parts(pre):
    normal_cdf = 0.5 * (1.0 + lax.erf(pre * SQRT_HALF))
    density = INV_ROOT_TAU * jnp.exp(-0.5 * pre * pre)
    return (pre * normal_cdf, normal_cdf + pre * density)


def iota(shape, dim):
    return lax.broadcasted_iota(jnp.int32, shape, dim)


def ones_where(mask):
    return jnp.where(mask, jnp.float32(1), jnp.float32(0)).astype(BF16)


def dot(a, b, dims=((1,), (0,))):
    return lax.dot_general(a, b, (dims, ((), ())), preferred_element_type=F32)


def kernel(
    n, n_model, tokens, grads, down_rows, up_rows, wanted, places, gates,
    input_grad, down_grad, up_grad,
    tok, grd, asked, table, sel_t, msg_out, msg_in, ret_out, ret_in,
    f_down, f_up, weight, coef_out, coef_in, coef_t, part_down, part_up,
    tok_sem, grd_sem, ask_send, ask_recv, row_send, row_recv, ret_send, ret_recv,
    down_send, down_recv, coef_send, coef_recv, self_sem,
):
    data_at = lax.axis_index("dp")
    model_at = lax.axis_index("mp")
    me = data_at * n_model + model_at
    rows, width = down_rows.shape
    capacity = ret_in.shape[0] // n // 8
    chunk = msg_out.shape[1]
    per_row = 2 * width // chunk
    message = capacity * per_row
    half = width // chunk
    slots = n * capacity
    n_tok = tok.shape[0]
    block = n_tok // n_model
    big = GROUP * message
    groups = n // GROUP

    def tok_copy(j):
        at = pl.ds(j * block, block)
        return pltpu.make_async_copy(tokens.at[at, :], tok.at[at, :], tok_sem.at[j])

    def grd_copy(j):
        at = pl.ds(j * block, block)
        return pltpu.make_async_copy(grads.at[at, :], grd.at[at, :], grd_sem.at[j])

    for j in range(n_model):
        tok_copy(j).start()
        grd_copy(j).start()

    def peer_of(k):
        peer = lax.rem(me + k, n)
        return peer, (lax.div(peer, n_model), lax.rem(peer, n_model))

    barrier = pltpu.get_barrier_semaphore()

    def greet(k, c):
        pl.semaphore_signal(barrier, inc=1, device_id=peer_of(k)[1], device_id_type=MESH)
        return c

    lax.fori_loop(1, n, greet, 0)

    for c in range(per_row):
        source = down_rows if c < half else up_rows
        at = (c % half) * chunk
        table[c * rows:(c + 1) * rows, :] = source[:, at:at + chunk]

    pl.semaphore_wait(barrier, n - 1)

    def ask_copy(k):
        peer, where = peer_of(k)
        return pltpu.make_async_remote_copy(
            src_ref=wanted.at[peer], dst_ref=asked.at[me], send_sem=ask_send.at[peer],
            recv_sem=ask_recv.at[me], device_id=where, device_id_type=MESH)

    def ask_start(k, c):
        ask_copy(k).start()
        return c

    lax.fori_loop(1, n, ask_start, 0)
    own_ask = pltpu.make_async_copy(wanted.at[me], asked.at[me], self_sem.at[0])
    own_ask.start()

    lanes = 256
    pairs = places.shape[0]

    def weigh(i, c):
        at = pl.ds(pl.multiple_of(i * lanes, lanes), lanes)
        for s0 in range(0, slots, 64):
            place = iota((64, lanes), 0) + s0
            total = jnp.zeros((64, lanes), F32)
            for p in range(pairs):
                total += jnp.where(places[p:p + 1, at] == place, gates[p:p + 1, at], jnp.float32(0))
            weight[s0:s0 + 64, at] = total
        return c

    lax.fori_loop(0, n_tok // lanes, weigh, 0)

    own_ask.wait()

    def ask_wait(k, c):
        src = lax.rem(me + n - k, n)
        pltpu.make_async_copy(asked.at[src], asked.at[src], ask_recv.at[src]).wait()
        return c

    lax.fori_loop(1, n, ask_wait, 0)

    def select(g):
        ask = asked[g * GROUP:(g + 1) * GROUP, 0, :].astype(F32)
        first = jnp.broadcast_to(ask[:, 0:1], (GROUP, 128))
        second = jnp.broadcast_to(ask[:, 64:65], (GROUP, 128))
        both = jnp.concatenate([first, second], axis=0)
        r = iota((big, capacity * GROUP), 0)
        c = iota((big, capacity * GROUP), 1)
        spread = ones_where(
            (lax.rem(c, GROUP) == lax.div(r, message))
            & (lax.div(c, GROUP) == lax.div(lax.rem(r, message), per_row)))
        wide = dot(spread, both.astype(BF16))
        lane = iota((big, 128), 1)
        value = wide.astype(jnp.int32)
        parts = []
        tiles = per_row * rows // 128
        for t in range(tiles):
            full = lane + t * 128
            hit = (lax.rem(full, rows) == value) & (
                lax.div(full, rows) == lax.rem(iota((big, 128), 0), per_row))
            parts.append(jnp.where(hit, jnp.float32(1), jnp.float32(0)))
        return jnp.concatenate(parts, axis=1)

    def row_copy(peer):
        at = pl.ds(pl.multiple_of(peer * message, message), message)
        mine = pl.ds(pl.multiple_of(me * message, message), message)
        return pltpu.make_async_remote_copy(
            src_ref=msg_out.at[at, :], dst_ref=msg_in.at[mine, :], send_sem=row_send.at[peer],
            recv_sem=row_recv.at[me],
            device_id=(lax.div(peer, n_model), lax.rem(peer, n_model)), device_id_type=MESH)

    mine_at = pl.ds(pl.multiple_of(me * message, message), message)
    own_row = pltpu.make_async_copy(msg_out.at[mine_at, :], msg_in.at[mine_at, :], self_sem.at[1])

    for g in range(groups):
        sel = select(g)
        sel_t[:, g * big:(g + 1) * big] = sel.T.astype(BF16)
        msg_out[g * big:(g + 1) * big, :] = dot(sel.astype(BF16), table[...]).astype(BF16)

    def row_start(k, c):
        row_copy(peer_of(k)[0]).start()
        return c

    lax.fori_loop(1, n, row_start, 0)
    own_row.start()
    own_row.wait()

    def row_wait(k, c):
        src = lax.rem(me + n - k, n)
        at = pl.ds(pl.multiple_of(src * message, message), message)
        pltpu.make_async_copy(msg_in.at[at, :], msg_in.at[at, :], row_recv.at[src]).wait()
        return c

    lax.fori_loop(1, n, row_wait, 0)

    seats = GROUP * capacity
    r = iota((big, big), 0)
    c = iota((big, big), 1)
    unpack = ones_where((lax.div(r, seats) == lax.rem(c, per_row)) & (lax.rem(r, seats) == lax.div(c, per_row)))
    pack = ones_where((lax.div(c, seats) == lax.rem(r, per_row)) & (lax.rem(c, seats) == lax.div(r, per_row)))
    own_down = pl.ds(pl.multiple_of(model_at * slots, slots), slots)
    for g in range(groups):
        laid = dot(unpack, msg_in[g * big:(g + 1) * big, :]).astype(BF16)
        for j in range(half):
            down_piece = laid[j * seats:(j + 1) * seats, :]
            up_piece = laid[(half + j) * seats:(half + j + 1) * seats, :]
            at = pl.ds(pl.multiple_of(model_at * slots + g * seats, seats), seats)
            f_down[at, j * chunk:(j + 1) * chunk] = down_piece
            f_up[g * seats:(g + 1) * seats, j * chunk:(j + 1) * chunk] = up_piece

    def down_copy(k):
        to = lax.rem(model_at + k, n_model)
        return pltpu.make_async_remote_copy(
            src_ref=f_down.at[own_down, :], dst_ref=f_down.at[own_down, :],
            send_sem=down_send.at[k], recv_sem=down_recv.at[k],
            device_id=(data_at, to), device_id_type=MESH)

    for k in range(1, n_model):
        down_copy(k).start()

    def coef_copy(j, k):
        return pltpu.make_async_remote_copy(
            src_ref=coef_out.at[j], dst_ref=coef_in.at[own_down, :],
            send_sem=coef_send.at[k], recv_sem=coef_recv.at[k],
            device_id=(data_at, j), device_id_type=MESH)

    for b in range(n_model):
        tok_copy(b).wait()
        grd_copy(b).wait()
        at = pl.ds(b * block, block)
        x = tok[at, :]
        y = grd[at, :]
        pre = dot(f_down[own_down, :], x, ((1,), (1,)))
        back = dot(f_up[...], y, ((1,), (1,)))
        w = weight[:, b * block:(b + 1) * block]
        active, slope = gelu_parts(pre)
        coef = (w * slope * back).astype(BF16)
        gated = (w * active).astype(BF16)
        coef_out[b] = coef
        if b == 0:
            part_down[...] = dot(coef, x)
            part_up[...] = dot(gated, y)
        else:
            part_down[...] += dot(coef, x)
            part_up[...] += dot(gated, y)

    for g in range(groups):
        pieces = []
        for source in (part_down, part_up):
            for j in range(half):
                pieces.append(source[g * seats:(g + 1) * seats, j * chunk:(j + 1) * chunk].astype(BF16))
        ret_out[g * big:(g + 1) * big, :] = dot(pack, jnp.concatenate(pieces, axis=0)).astype(BF16)

    def ret_copy(peer):
        at = pl.ds(pl.multiple_of(peer * message, message), message)
        return pltpu.make_async_remote_copy(
            src_ref=ret_out.at[at, :], dst_ref=ret_in.at[mine_at, :], send_sem=ret_send.at[peer],
            recv_sem=ret_recv.at[me],
            device_id=(lax.div(peer, n_model), lax.rem(peer, n_model)), device_id_type=MESH)

    for k in range(1, n_model):
        coef_copy(lax.rem(model_at + k, n_model), k).start()

    def ret_start(k, c):
        ret_copy(peer_of(k)[0]).start()
        return c

    lax.fori_loop(1, n, ret_start, 0)
    own_ret = pltpu.make_async_copy(ret_out.at[mine_at, :], ret_in.at[mine_at, :], self_sem.at[2])
    own_ret.start()

    own_coef = pltpu.make_async_copy(coef_out.at[model_at], coef_in.at[own_down, :], self_sem.at[3])
    own_coef.start()
    own_coef.wait()
    for k in range(1, n_model):
        frm = lax.rem(model_at + n_model - k, n_model)
        there = pl.ds(pl.multiple_of(frm * slots, slots), slots)
        pltpu.make_async_copy(coef_in.at[there, :], coef_in.at[there, :], coef_recv.at[k]).wait()
        pltpu.make_async_copy(f_down.at[there, :], f_down.at[there, :], down_recv.at[k]).wait()
    coef_t[...] = coef_in[...].astype(F32).T.astype(BF16)

    def finish(i, c):
        at = pl.ds(pl.multiple_of(i * 512, 512), 512)
        input_grad[:, at] = dot(coef_t[...], f_down[:, at]).astype(BF16)
        return c

    lax.fori_loop(0, width // 512, finish, 0)

    own_ret.wait()

    def ret_wait(k, c):
        src = lax.rem(me + n - k, n)
        at = pl.ds(pl.multiple_of(src * message, message), message)
        pltpu.make_async_copy(ret_in.at[at, :], ret_in.at[at, :], ret_recv.at[src]).wait()
        return c

    lax.fori_loop(1, n, ret_wait, 0)
    for c in range(per_row):
        target = down_grad if c < half else up_grad
        at = (c % half) * chunk
        target[:, at:at + chunk] = dot(sel_t[c * rows:(c + 1) * rows, :], ret_in[...])

    def sent(k, c):
        peer = peer_of(k)[0]
        ask_copy(k).wait_send()
        row_copy(peer).wait_send()
        ret_copy(peer).wait_send()
        return c

    lax.fori_loop(1, n, sent, 0)
    for k in range(1, n_model):
        down_copy(k).wait_send()
        coef_copy(lax.rem(model_at + k, n_model), k).wait_send()


def shards(tokens, out_grad, down_rows, up_rows, requests, places, gate_weights):
    n_model = lax.axis_size("mp")
    n = lax.axis_size("dp") * n_model
    rows, width = down_rows.shape
    n_tok = tokens.shape[0]
    slots = requests.shape[1] * requests.shape[2]
    block = n_tok // n_model
    chunk = 2 * width // 8
    message = requests.shape[2] * 8
    wanted = jnp.repeat(requests[0], 64, axis=1)[:, None, :]
    chosen = jnp.transpose(places, (0, 2, 1)).reshape(-1, n_tok)
    gates = jnp.transpose(gate_weights, (0, 2, 1)).reshape(-1, n_tok)
    vmem = pl.BlockSpec(memory_space=pltpu.VMEM)
    hbm = pl.BlockSpec(memory_space=pl.ANY)
    dma = pltpu.SemaphoreType.DMA
    flops = 10 * n_tok * slots * width
    return pl.pallas_call(
        functools.partial(kernel, n, n_model),
        out_shape=(
            jax.ShapeDtypeStruct((block, width), BF16),
            jax.ShapeDtypeStruct((rows, width), F32),
            jax.ShapeDtypeStruct((rows, width), F32),
        ),
        in_specs=[hbm, hbm, vmem, vmem, vmem, vmem, vmem],
        out_specs=(vmem, vmem, vmem),
        scratch_shapes=[
            pltpu.VMEM((n_tok, width), BF16),
            pltpu.VMEM((n_tok, width), BF16),
            pltpu.VMEM((n, 1, 128), jnp.int32),
            pltpu.VMEM((8 * rows, chunk), BF16),
            pltpu.VMEM((8 * rows, n * message), BF16),
            pltpu.VMEM((n * message, chunk), BF16),
            pltpu.VMEM((n * message, chunk), BF16),
            pltpu.VMEM((n * message, chunk), BF16),
            pltpu.VMEM((n * message, chunk), BF16),
            pltpu.VMEM((n_model * slots, width), BF16),
            pltpu.VMEM((slots, width), BF16),
            pltpu.VMEM((slots, n_tok), F32),
            pltpu.VMEM((n_model, slots, block), BF16),
            pltpu.VMEM((n_model * slots, block), BF16),
            pltpu.VMEM((block, n_model * slots), BF16),
            pltpu.VMEM((slots, width), F32),
            pltpu.VMEM((slots, width), F32),
            dma((n_model,)), dma((n_model,)),
            dma((n,)), dma((n,)), dma((n,)), dma((n,)), dma((n,)), dma((n,)),
            dma((n_model,)), dma((n_model,)), dma((n_model,)), dma((n_model,)),
            dma((4,)),
        ],
        compiler_params=pltpu.CompilerParams(
            collective_id=0, has_side_effects=True, vmem_limit_bytes=60 * 1024 * 1024),
        cost_estimate=pl.CostEstimate(
            flops=flops, bytes_accessed=4 * n_tok * width, transcendentals=2 * n_tok * slots),
    )(tokens, out_grad, down_rows, up_rows, wanted, chosen, gates)


def solution(mesh):
    in_specs = (
        P("dp", None),
        P("dp", None),
        P(("dp", "mp"), None),
        P(("dp", "mp"), None),
        P(("dp", "mp"), None, None),
        P("mp", "dp", None),
        P("mp", "dp", None),
    )
    out_specs = (P(("dp", "mp"), None), P(("dp", "mp"), None), P(("dp", "mp"), None))
    return jax.shard_map(shards, mesh=mesh, in_specs=in_specs, out_specs=out_specs, check_vma=False)
```

time: 143 us -> 61.3 us (0.43)
  the two profiles are of different devices: /device:TPU:0 before, /device:TPU:11 now
where the time goes in v2:
time: 61.3 us; the launch traced here: 61 us
  Pallas kernels  51.9 us (85%)
  local copies, waits for them, and re-layouts  8.46 us (14%)
  between operations  0.65 us (1%)
    pallas_call x1, Pallas kernels, shards(): pl.pallas_call(functools.partial(kernel, n, n_model), out_shape=(jax.Shap...  51.9 us
    unnamed x3, local copies, waits for them, and re-layouts  6.9 us

profile of v2, /device:TPU:11, one launch (start us, length us, event | category | flops | bytes accessed | tf_op | source)
XLA Modules:
  0.0 61.0 jit_solution(5608386647181801015)
XLA Ops:
  0.6 0.8 %copy.10 = s32[32,2]{1,0:T(8,128)S(1)} copy(s32[32,2]{0,1:T(2,128)} %bitcast.9) | data formatting | bytes 512 | tf_op jit(solution)/shard_map/squeeze | solution.py:311
  1.4 0.1 broadcast_in_dim.3
  1.5 0.7 %broadcast_in_dim_reshape.3.wanted = s32[32,1,128]{2,1,0:T(1,128)} reshape(s32[32,2,64]{2,1,0:T(2,128)S(1)} %broadcast_in_dim.3) | data formatting | bytes 32768 | tf_op jit(solution)/shard_map/broadcast_in_dim;reshape | solution.py:311
  2.2 51.9 %shard_map.94 = (bf16[512,2048]{1,0:T(8,128)(2,1)}, f32[64,2048]{1,0:T(8,128)}, f32[64,2048]{1,0:T(8,128)}) custom-call(bf16[2048,2048]{1,0:T(8,128)(2,1)} %tokens.1, bf16[2048,2048]{1,0:T(8,128)(2,1)} %grads.1, bf16[64,2048]{1,0:T(8,128)(2,1)} %down_rows.1, bf16[64,2048]{1,0:T(8,128)(2,1)} %up_rows.1, s32[32,1,128]{2,1,0:T(1,128)} %broadcast_in_dim_reshape.3.wanted, ...), custom_call_target="tpu_custom_call" | custom-call | flops 2684354560 | bytes 16777216 | tf_op jit(solution)/shard_map/pallas_call | solution.py:318
  54.1 3.2 %copy.14 = bf16[512,2048]{1,0:T(8,128)(2,1)} copy(bf16[512,2048]{1,0:T(8,128)(2,1)} %get-tuple-element.6) | data formatting | bytes 4194304
  57.2 1.9 %copy.15 = f32[64,2048]{1,0:T(8,128)} copy(f32[64,2048]{1,0:T(8,128)} %get-tuple-element.7) | data formatting | bytes 1048576
  59.1 1.9 %copy.16 = f32[64,2048]{1,0:T(8,128)} copy(f32[64,2048]{1,0:T(8,128)} %get-tuple-element.8) | data formatting | bytes 1048576

commit v3 on v2

v3 whole, which is shorter than its diff:
```python
import functools
import math

import jax
import jax.numpy as jnp
from jax import lax
from jax.experimental import pallas as pl
from jax.experimental.pallas import tpu as pltpu
from jax.sharding import PartitionSpec as P

SQRT_HALF = 0.7071067811865476
INV_ROOT_TAU = 0.3989422804014327
F32 = jnp.float32
BF16 = jnp.bfloat16
GROUP = 8
PIECES = 8
SPARE = 4 * 1024 * 1024
MESH = pl.DeviceIdType.MESH


def gelu_parts(pre):
    normal_cdf = 0.5 * (1.0 + lax.erf(pre * SQRT_HALF))
    density = INV_ROOT_TAU * jnp.exp(-0.5 * pre * pre)
    return (pre * normal_cdf, normal_cdf + pre * density)


def iota(shape, dim):
    return lax.broadcasted_iota(jnp.int32, shape, dim)


def ones_where(mask):
    return jnp.where(mask, jnp.float32(1), jnp.float32(0)).astype(BF16)


def dot(a, b, dims=((1,), (0,))):
    return lax.dot_general(a, b, (dims, ((), ())), preferred_element_type=F32)


def kernel(
    n, n_model, tokens, grads, down_rows, up_rows, requests, places, gates,
    input_grad, down_grad, up_grad,
    tok, grd, pad, wanted, asked, table, sel, sel_t, msg_out, msg_in, ret_out, ret_in,
    f_down, f_up, weight, gated, coef_out, coef_in, coef_t, part,
    tok_sem, grd_sem, ask_send, ask_recv, row_send, row_recv, ret_send, ret_recv,
    down_send, down_recv, coef_send, coef_recv,
):
    data_at = lax.axis_index("dp")
    model_at = lax.axis_index("mp")
    me = data_at * n_model + model_at
    rows, width = down_rows.shape
    capacity = requests.shape[0]
    per_row = PIECES
    chunk = width // per_row
    message = capacity * per_row
    slots = n * capacity
    n_tok = tok.shape[0]
    block = n_tok // n_model
    big = GROUP * message
    groups = n // GROUP
    lines = n_model // 2

    def tok_copy(j):
        at = pl.ds(j * block, block)
        return pltpu.make_async_copy(tokens.at[at, :], tok.at[at, :], tok_sem.at[j])

    def grd_copy(j):
        at = pl.ds(j * block, block)
        return pltpu.make_async_copy(grads.at[at, :], grd.at[at, :], grd_sem.at[j])

    for j in range(n_model):
        tok_copy(j).start()
    for j in range(n_model):
        grd_copy(j).start()

    def where(peer):
        return (lax.div(peer, n_model), lax.rem(peer, n_model))

    def peer_of(k):
        return lax.rem(me + k, n)

    barrier = pltpu.get_barrier_semaphore()

    def greet(k, c):
        pl.semaphore_signal(barrier, inc=1, device_id=where(peer_of(k)), device_id_type=MESH)
        return c

    lax.fori_loop(1, n, greet, 0)

    pad[...] = jnp.zeros_like(pad)
    pad[0:capacity, 0:n] = requests[...]
    turned = pad[...].T
    span = 128 // capacity
    wanted[:, 0, :] = jnp.concatenate(
        [jnp.broadcast_to(turned[0:n, r:r + 1], (n, span)) for r in range(capacity)], axis=1)

    for kind, source in enumerate((down_rows, up_rows)):
        for c in range(per_row):
            table[kind, c * rows:(c + 1) * rows, :] = source[:, c * chunk:(c + 1) * chunk]

    pl.semaphore_wait(barrier, n - 1)

    def ask_copy(peer):
        return pltpu.make_async_remote_copy(
            src_ref=wanted.at[peer], dst_ref=asked.at[me], send_sem=ask_send.at[peer],
            recv_sem=ask_recv.at[me], device_id=where(peer), device_id_type=MESH)

    def ask_start(k, c):
        ask_copy(peer_of(k)).start()
        return c

    lax.fori_loop(1, n, ask_start, 0)
    pltpu.make_async_copy(wanted.at[me], asked.at[me], ask_recv.at[me]).start()

    lanes = 256
    pairs = places.shape[0]

    def weigh(i, c):
        at = pl.ds(pl.multiple_of(i * lanes, lanes), lanes)
        for s0 in range(0, slots, 64):
            place = iota((64, lanes), 0) + s0
            total = jnp.zeros((64, lanes), F32)
            for p in range(pairs):
                total += jnp.where(places[p:p + 1, at] == place, gates[p:p + 1, at], jnp.float32(0))
            weight[s0:s0 + 64, at] = total
        return c

    lax.fori_loop(0, n_tok // lanes, weigh, 0)

    def select(g):
        ask = asked[g * GROUP:(g + 1) * GROUP, 0, :].astype(F32)
        both = jnp.concatenate(
            [jnp.broadcast_to(ask[:, r * span:r * span + 1], (GROUP, 128)) for r in range(capacity)], axis=0)
        r = iota((big, capacity * GROUP), 0)
        c = iota((big, capacity * GROUP), 1)
        spread = ones_where(
            (lax.rem(c, GROUP) == lax.div(r, message))
            & (lax.div(c, GROUP) == lax.div(lax.rem(r, message), per_row)))
        value = dot(spread, both.astype(BF16)).astype(jnp.int32)
        lane = iota((big, 128), 1)
        piece = lax.rem(iota((big, 128), 0), per_row)
        parts = []
        for t in range(per_row * rows // 128):
            full = lane + t * 128
            hit = (lax.rem(full, rows) == value) & (lax.div(full, rows) == piece)
            parts.append(jnp.where(hit, jnp.float32(1), jnp.float32(0)))
        return jnp.concatenate(parts, axis=1)

    def span_of(peer):
        return pl.ds(pl.multiple_of(peer * message, message), message)

    def exchange(source, target, send, recv, kind):
        def remote(peer):
            return pltpu.make_async_remote_copy(
                src_ref=source.at[kind, span_of(peer), :], dst_ref=target.at[kind, span_of(me), :],
                send_sem=send.at[kind, peer], recv_sem=recv.at[kind, me],
                device_id=where(peer), device_id_type=MESH)

        def start(i, c):
            @pl.when(i != me)
            def _():
                remote(i).start()

            @pl.when(i == me)
            def _():
                pltpu.make_async_copy(
                    source.at[kind, span_of(me), :], target.at[kind, span_of(me), :],
                    recv.at[kind, me]).start()
            return c

        def start_all(k, c):
            remote(peer_of(k)).start()
            return c

        def arrive(i, c):
            at = target.at[kind, span_of(i), :]
            pltpu.make_async_copy(at, at, recv.at[kind, i]).wait()
            return c

        def sent(k, c):
            remote(peer_of(k)).wait_send()
            return c

        def begin():
            lax.fori_loop(1, n, start_all, 0)
            pltpu.make_async_copy(
                source.at[kind, span_of(me), :], target.at[kind, span_of(me), :],
                recv.at[kind, me]).start()

        return (
            lambda g: lax.fori_loop(g * GROUP, (g + 1) * GROUP, start, 0),
            begin,
            lambda g: lax.fori_loop(g * GROUP, (g + 1) * GROUP, arrive, 0),
            lambda: lax.fori_loop(1, n, sent, 0),
        )

    row_moves = [exchange(msg_out, msg_in, row_send, row_recv, kind) for kind in range(2)]
    ret_moves = [exchange(ret_out, ret_in, ret_send, ret_recv, kind) for kind in range(2)]

    def ask_wait(i, c):
        pltpu.make_async_copy(asked.at[i], asked.at[i], ask_recv.at[i]).wait()
        return c

    for g in range(groups):
        at = slice(g * big, (g + 1) * big)
        lax.fori_loop(g * GROUP, (g + 1) * GROUP, ask_wait, 0)
        sel[at, :] = select(g)
        msg_out[0, at, :] = dot(sel[at, :].astype(BF16), table[0]).astype(BF16)
        row_moves[0][0](g)
    for g in range(groups):
        at = slice(g * big, (g + 1) * big)
        msg_out[1, at, :] = dot(sel[at, :].astype(BF16), table[1]).astype(BF16)
        row_moves[1][0](g)
    for g in range(groups):
        at = slice(g * big, (g + 1) * big)
        sel_t[:, at] = sel[at, :].T.astype(BF16)

    seats = GROUP * capacity
    r = iota((big, big), 0)
    c = iota((big, big), 1)
    unpack = ones_where(
        (lax.div(r, seats) == lax.rem(c, per_row)) & (lax.rem(r, seats) == lax.div(c, per_row)))
    pack = ones_where(
        (lax.div(c, seats) == lax.rem(r, per_row)) & (lax.rem(c, seats) == lax.div(r, per_row)))

    def fetch(kind, target, base):
        for g in range(groups):
            row_moves[kind][2](g)
            laid = dot(unpack, msg_in[kind, g * big:(g + 1) * big, :]).astype(BF16)
            at = pl.ds(pl.multiple_of(base + g * seats, seats), seats)
            for j in range(per_row):
                target[at, j * chunk:(j + 1) * chunk] = laid[j * seats:(j + 1) * seats, :]

    def put_back(kind):
        for g in range(groups):
            pieces = [
                part[kind, g * seats:(g + 1) * seats, j * chunk:(j + 1) * chunk].astype(BF16)
                for j in range(per_row)
            ]
            ret_out[kind, g * big:(g + 1) * big, :] = dot(
                pack, jnp.concatenate(pieces, axis=0)).astype(BF16)
        ret_moves[kind][1]()

    def slots_of(q):
        return pl.ds(pl.multiple_of(q * slots, slots), slots)

    own = slots_of(model_at)
    sibling = model_at + 1 - 2 * lax.rem(model_at, 2)

    def down_copy(q, to, sem):
        return pltpu.make_async_remote_copy(
            src_ref=f_down.at[slots_of(q), :], dst_ref=f_down.at[slots_of(q), :],
            send_sem=down_send.at[sem], recv_sem=down_recv.at[q],
            device_id=(data_at, to), device_id_type=MESH)

    def same_core(j):
        return lax.rem(model_at + 2 * j, n_model)

    def down_wait(q):
        at = f_down.at[slots_of(q), :]
        pltpu.make_async_copy(at, at, down_recv.at[q]).wait()

    fetch(0, f_down, model_at * slots)
    for j in range(1, lines):
        down_copy(model_at, same_core(j), j).start()
    down_copy(model_at, sibling, 0).start()

    for b in range(n_model):
        at = slice(b * block, (b + 1) * block)
        tok_copy(b).wait()
        pre = dot(f_down[own, :], tok[at, :], ((1,), (1,)))
        active, slope = gelu_parts(pre)
        w = weight[:, at]
        gated[:, at] = (w * active).astype(BF16)
        weight[:, at] = w * slope
    for b in range(n_model):
        grd_copy(b).wait()
    step = 512
    for c0 in range(0, width, step):
        part[1, :, c0:c0 + step] = dot(gated[...], grd[:, c0:c0 + step])
    put_back(1)

    for j in range(1, lines):
        down_wait(same_core(j))
        down_copy(same_core(j), sibling, lines + j).start()

    fetch(1, f_up, 0)
    for b in range(n_model):
        at = slice(b * block, (b + 1) * block)
        back = dot(f_up[...], grd[at, :], ((1,), (1,)))
        coef = (weight[:, at] * back).astype(BF16)
        coef_out[b] = coef
        gated[:, at] = coef

    def coef_copy(j, k):
        return pltpu.make_async_remote_copy(
            src_ref=coef_out.at[j], dst_ref=coef_in.at[own, :],
            send_sem=coef_send.at[k], recv_sem=coef_recv.at[k],
            device_id=(data_at, j), device_id_type=MESH)

    for k in range(1, n_model):
        coef_copy(lax.rem(model_at + k, n_model), k).start()
    own_coef = pltpu.make_async_copy(coef_out.at[model_at], coef_in.at[own, :], coef_recv.at[0])
    own_coef.start()

    for c0 in range(0, width, step):
        part[0, :, c0:c0 + step] = dot(gated[...], tok[:, c0:c0 + step])
    put_back(0)

    down_wait(sibling)
    for j in range(1, lines):
        down_wait(lax.rem(sibling + 2 * j, n_model))
    own_coef.wait()
    for k in range(1, n_model):
        there = coef_in.at[slots_of(lax.rem(model_at + n_model - k, n_model)), :]
        pltpu.make_async_copy(there, there, coef_recv.at[k]).wait()
    coef_t[...] = coef_in[...].astype(F32).T.astype(BF16)

    def finish(i, c):
        at = pl.ds(pl.multiple_of(i * step, step), step)
        input_grad[:, at] = dot(coef_t[...], f_down[:, at]).astype(BF16)
        return c

    lax.fori_loop(0, width // step, finish, 0)

    for kind, target in ((1, up_grad), (0, down_grad)):
        for g in range(groups):
            ret_moves[kind][2](g)
        for c0 in range(per_row):
            target[:, c0 * chunk:(c0 + 1) * chunk] = dot(
                sel_t[c0 * rows:(c0 + 1) * rows, :], ret_in[kind])

    def ask_sent(k, c):
        ask_copy(peer_of(k)).wait_send()
        return c

    lax.fori_loop(1, n, ask_sent, 0)
    for kind in range(2):
        row_moves[kind][3]()
        ret_moves[kind][3]()
    down_copy(model_at, sibling, 0).wait_send()
    for j in range(1, lines):
        down_copy(model_at, same_core(j), j).wait_send()
        down_copy(same_core(j), sibling, lines + j).wait_send()
    for k in range(1, n_model):
        coef_copy(lax.rem(model_at + k, n_model), k).wait_send()


def shards(tokens, out_grad, down_rows, up_rows, requests, places, gate_weights):
    n_model = lax.axis_size("mp")
    n = lax.axis_size("dp") * n_model
    rows, width = down_rows.shape
    n_tok = tokens.shape[0]
    capacity = requests.shape[2]
    slots = n * capacity
    block = n_tok // n_model
    chunk = width // PIECES
    moved = n * capacity * PIECES
    wanted = jnp.transpose(requests[0], (1, 0))
    chosen = jnp.transpose(places, (0, 2, 1)).reshape(-1, n_tok)
    gates = jnp.transpose(gate_weights, (0, 2, 1)).reshape(-1, n_tok)
    vmem = pl.BlockSpec(memory_space=pltpu.VMEM)
    hbm = pl.BlockSpec(memory_space=pltpu.HBM)
    dma = pltpu.SemaphoreType.DMA
    flops = 10 * n_tok * slots * width
    buffers = [
        ((n_tok, width), BF16),
        ((n_tok, width), BF16),
        ((128, 128), jnp.int32),
        ((n, 1, 128), jnp.int32),
        ((n, 1, 128), jnp.int32),
        ((2, PIECES * rows, chunk), BF16),
        ((moved, PIECES * rows), F32),
        ((PIECES * rows, moved), BF16),
        ((2, moved, chunk), BF16),
        ((2, moved, chunk), BF16),
        ((2, moved, chunk), BF16),
        ((2, moved, chunk), BF16),
        ((n_model * slots, width), BF16),
        ((slots, width), BF16),
        ((slots, n_tok), F32),
        ((slots, n_tok), BF16),
        ((n_model, slots, block), BF16),
        ((n_model * slots, block), BF16),
        ((block, n_model * slots), BF16),
        ((2, slots, width), F32),
    ]
    taken = sum(math.prod(shape) * jnp.dtype(kind).itemsize for shape, kind in buffers)
    ends = block * width * 2 + rows * width * 12 + chosen.size * 8
    return pl.pallas_call(
        functools.partial(kernel, n, n_model),
        out_shape=(
            jax.ShapeDtypeStruct((block, width), BF16),
            jax.ShapeDtypeStruct((rows, width), F32),
            jax.ShapeDtypeStruct((rows, width), F32),
        ),
        in_specs=[hbm, hbm, vmem, vmem, vmem, vmem, vmem],
        out_specs=(vmem, vmem, vmem),
        scratch_shapes=[pltpu.VMEM(shape, kind) for shape, kind in buffers] + [
            dma((n_model,)), dma((n_model,)), dma((n,)), dma((n,)),
            dma((2, n)), dma((2, n)), dma((2, n)), dma((2, n)),
            dma((n_model,)), dma((n_model,)), dma((n_model,)), dma((n_model,)),
        ],
        compiler_params=pltpu.CompilerParams(
            collective_id=0, has_side_effects=True, vmem_limit_bytes=taken + ends + SPARE),
        cost_estimate=pl.CostEstimate(
            flops=flops, bytes_accessed=4 * n_tok * width, transcendentals=2 * n_tok * slots),
    )(tokens, out_grad, down_rows, up_rows, wanted, chosen, gates)


def solution(mesh):
    in_specs = (
        P("dp", None),
        P("dp", None),
        P(("dp", "mp"), None),
        P(("dp", "mp"), None),
        P(("dp", "mp"), None, None),
        P("mp", "dp", None),
        P("mp", "dp", None),
    )
    out_specs = (P(("dp", "mp"), None), P(("dp", "mp"), None), P(("dp", "mp"), None))
    return jax.shard_map(shards, mesh=mesh, in_specs=in_specs, out_specs=out_specs, check_vma=False)
```

time: 61.3 us -> 64.3 us (1.049)
  the two profiles are of different devices: /device:TPU:11 before, /device:TPU:0 now
where the time goes in v3:
time: 64.3 us; the launch traced here: 64 us
  Pallas kernels  49.2 us (77%)
  local copies, waits for them, and re-layouts  14.1 us (22%)
  between operations  0.66 us (1%)
    pallas_call x1, Pallas kernels, shards(): pl.pallas_call(functools.partial(kernel, n, n_model), out_shape=(jax.Shap...  49.2 us
    unnamed x17, local copies, waits for them, and re-layouts  14.1 us

profile of v3, /device:TPU:0, one launch (start us, length us, event | category | flops | bytes accessed | tf_op | source)
XLA Modules:
  0.0 64.0 jit_solution(14279998952473162108)
XLA Ops:
  0.6 0.0 copy-start
  0.6 3.4 %copy-done = bf16[2048,2048]{1,0:T(8,128)(2,1)S(1)} copy-done((bf16[2048,2048]{1,0:T(8,128)(2,1)S(1)}, bf16[2048,2048]{1,0:T(8,128)(2,1)}, u32[]{:S(2)}) %copy-start) | copy-done | bytes 8388632
  4.0 0.0 copy-start.1
  4.0 3.4 %copy-done.1 = bf16[2048,2048]{1,0:T(8,128)(2,1)S(1)} copy-done((bf16[2048,2048]{1,0:T(8,128)(2,1)S(1)}, bf16[2048,2048]{1,0:T(8,128)(2,1)}, u32[]{:S(2)}) %copy-start.1) | copy-done | bytes 8388632
  7.4 0.0 copy-start.2
  7.4 0.9 %copy-done.2 = bf16[64,2048]{1,0:T(8,128)(2,1)S(1)} copy-done((bf16[64,2048]{1,0:T(8,128)(2,1)S(1)}, bf16[64,2048]{1,0:T(8,128)(2,1)}, u32[]{:S(2)}) %copy-start.2) | copy-done | bytes 262168
  8.3 0.0 copy-start.3
  8.3 0.9 %copy-done.3 = bf16[64,2048]{1,0:T(8,128)(2,1)S(1)} copy-done((bf16[64,2048]{1,0:T(8,128)(2,1)S(1)}, bf16[64,2048]{1,0:T(8,128)(2,1)}, u32[]{:S(2)}) %copy-start.3) | copy-done | bytes 262168
  9.3 0.0 copy-start.4
  9.3 0.9 %copy-done.4 = s32[2,2048,16]{1,2,0:T(8,128)S(1)} copy-done((s32[2,2048,16]{1,2,0:T(8,128)S(1)}, s32[2,2048,16]{1,2,0:T(8,128)}, u32[]{:S(2)}) %copy-start.4) | copy-done | bytes 262168
  10.2 0.0 copy-start.5
  10.3 0.9 %copy-done.5 = f32[2,2048,16]{1,2,0:T(8,128)S(1)} copy-done((f32[2,2048,16]{1,2,0:T(8,128)S(1)}, f32[2,2048,16]{1,2,0:T(8,128)}, u32[]{:S(2)}) %copy-start.5) | copy-done | bytes 262168
  11.2 0.0 copy-start.6
  11.2 0.7 %copy-done.6 = s32[1,32,2]{1,2,0:T(2,128)S(1)} copy-done((s32[1,32,2]{1,2,0:T(2,128)S(1)}, s32[1,32,2]{1,2,0:T(2,128)}, u32[]{:S(2)}) %copy-start.6) | copy-done | bytes 280
  11.9 49.2 %shard_map.94 = (bf16[512,2048]{1,0:T(8,128)(2,1)S(1)}, f32[64,2048]{1,0:T(8,128)S(1)}, f32[64,2048]{1,0:T(8,128)S(1)}) custom-call(bf16[2048,2048]{1,0:T(8,128)(2,1)S(1)} %copy-done, bf16[2048,2048]{1,0:T(8,128)(2,1)S(1)} %copy-done.1, bf16[64,2048]{1,0:T(8,128)(2,1)S(1)} %copy-done.2, bf16[64,2048]{1,0:T(8,128)(2,1)S(1)} %copy-done.3, ...), custom_call_target="tpu_custom_call" | custom-call | flops 2684354560 | bytes 16777216 | tf_op jit(solution)/shard_map/pallas_call | solution.py:389
  61.1 1.3 %copy.13 = bf16[512,2048]{1,0:T(8,128)(2,1)} copy(bf16[512,2048]{1,0:T(8,128)(2,1)S(1)} %get-tuple-element.6) | data formatting | bytes 4194304
  62.4 0.8 %copy.14 = f32[64,2048]{1,0:T(8,128)} copy(f32[64,2048]{1,0:T(8,128)S(1)} %get-tuple-element.7) | data formatting | bytes 1048576
  63.2 0.8 %copy.15 = f32[64,2048]{1,0:T(8,128)} copy(f32[64,2048]{1,0:T(8,128)S(1)} %get-tuple-element.8) | data formatting | bytes 1048576
Async XLA Ops:
  0.6 3.4 %copy-start = (bf16[2048,2048]{1,0:T(8,128)(2,1)S(1)}, bf16[2048,2048]{1,0:T(8,128)(2,1)}, u32[]{:S(2)}) copy-start(bf16[2048,2048]{1,0:T(8,128)(2,1)} %tokens.1) | copy-start | bytes 25165828
  4.0 3.4 %copy-start.1 = (bf16[2048,2048]{1,0:T(8,128)(2,1)S(1)}, bf16[2048,2048]{1,0:T(8,128)(2,1)}, u32[]{:S(2)}) copy-start(bf16[2048,2048]{1,0:T(8,128)(2,1)} %grads.1) | copy-start | bytes 25165828
  7.4 0.9 %copy-start.2 = (bf16[64,2048]{1,0:T(8,128)(2,1)S(1)}, bf16[64,2048]{1,0:T(8,128)(2,1)}, u32[]{:S(2)}) copy-start(bf16[64,2048]{1,0:T(8,128)(2,1)} %down_rows.1) | copy-start | bytes 786436
  8.3 0.9 %copy-start.3 = (bf16[64,2048]{1,0:T(8,128)(2,1)S(1)}, bf16[64,2048]{1,0:T(8,128)(2,1)}, u32[]{:S(2)}) copy-start(bf16[64,2048]{1,0:T(8,128)(2,1)} %up_rows.1) | copy-start | bytes 786436
  9.3 0.9 %copy-start.4 = (s32[2,2048,16]{1,2,0:T(8,128)S(1)}, s32[2,2048,16]{1,2,0:T(8,128)}, u32[]{:S(2)}) copy-start(s32[2,2048,16]{1,2,0:T(8,128)} %param.12) | copy-start | bytes 786436
  10.2 0.9 %copy-start.5 = (f32[2,2048,16]{1,2,0:T(8,128)S(1)}, f32[2,2048,16]{1,2,0:T(8,128)}, u32[]{:S(2)}) copy-start(f32[2,2048,16]{1,2,0:T(8,128)} %param.13) | copy-start | bytes 786436
  11.2 0.7 %copy-start.6 = (s32[1,32,2]{1,2,0:T(2,128)S(1)}, s32[1,32,2]{1,2,0:T(2,128)}, u32[]{:S(2)}) copy-start(s32[1,32,2]{1,2,0:T(2,128)} %param.11) | copy-start | bytes 772

commit v4 on v3

--- a/solution.py
+++ b/solution.py
@@ -15,6 +15,7 @@
 GROUP = 8
 PIECES = 8
 SPARE = 4 * 1024 * 1024
+GRANT = 46 * 1024 * 1024
 MESH = pl.DeviceIdType.MESH
 
 
@@ -26,6 +27,18 @@
 
 def iota(shape, dim):
     return lax.broadcasted_iota(jnp.int32, shape, dim)
+
+
+def div(values, by):
+    if by & (by - 1) == 0:
+        return lax.shift_right_logical(values, jnp.full_like(values, by.bit_length() - 1))
+    return lax.div(values, by)
+
+
+def rem(values, by):
+    if by & (by - 1) == 0:
+        return values & (by - 1)
+    return lax.rem(values, by)
 
 
 def ones_where(mask):
@@ -72,19 +85,25 @@
     for j in range(n_model):
         grd_copy(j).start()
 
-    def where(peer):
-        return (lax.div(peer, n_model), lax.rem(peer, n_model))
-
-    def peer_of(k):
-        return lax.rem(me + k, n)
+    n_data = n // n_model
+
+    def others(act):
+        def line(k, c):
+            p = data_at + k
+            p = jnp.where(p >= n_data, p - n_data, p)
+            for q in range(n_model):
+                peer = p * n_model + q
+
+                @pl.when(peer != me)
+                def _():
+                    act(peer, (p, q))
+            return c
+
+        lax.fori_loop(0, n_data, line, 0)
 
     barrier = pltpu.get_barrier_semaphore()
-
-    def greet(k, c):
-        pl.semaphore_signal(barrier, inc=1, device_id=where(peer_of(k)), device_id_type=MESH)
-        return c
-
-    lax.fori_loop(1, n, greet, 0)
+    others(lambda peer, to: pl.semaphore_signal(
+        barrier, inc=1, device_id=to, device_id_type=MESH))
 
     pad[...] = jnp.zeros_like(pad)
     pad[0:capacity, 0:n] = requests[...]
@@ -99,16 +118,12 @@
 
     pl.semaphore_wait(barrier, n - 1)
 
-    def ask_copy(peer):
+    def ask_copy(peer, to):
         return pltpu.make_async_remote_copy(
             src_ref=wanted.at[peer], dst_ref=asked.at[me], send_sem=ask_send.at[peer],
-            recv_sem=ask_recv.at[me], device_id=where(peer), device_id_type=MESH)
-
-    def ask_start(k, c):
-        ask_copy(peer_of(k)).start()
-        return c
-
-    lax.fori_loop(1, n, ask_start, 0)
+            recv_sem=ask_recv.at[me], device_id=to, device_id_type=MESH)
+
+    others(lambda peer, to: ask_copy(peer, to).start())
     pltpu.make_async_copy(wanted.at[me], asked.at[me], ask_recv.at[me]).start()
 
     lanes = 256
@@ -133,15 +148,15 @@
         r = iota((big, capacity * GROUP), 0)
         c = iota((big, capacity * GROUP), 1)
         spread = ones_where(
-            (lax.rem(c, GROUP) == lax.div(r, message))
-            & (lax.div(c, GROUP) == lax.div(lax.rem(r, message), per_row)))
+            (rem(c, GROUP) == div(r, message))
+            & (div(c, GROUP) == div(rem(r, message), per_row)))
         value = dot(spread, both.astype(BF16)).astype(jnp.int32)
         lane = iota((big, 128), 1)
-        piece = lax.rem(iota((big, 128), 0), per_row)
+        piece = rem(iota((big, 128), 0), per_row)
         parts = []
         for t in range(per_row * rows // 128):
             full = lane + t * 128
-            hit = (lax.rem(full, rows) == value) & (lax.div(full, rows) == piece)
+            hit = (rem(full, rows) == value) & (div(full, rows) == piece)
             parts.append(jnp.where(hit, jnp.float32(1), jnp.float32(0)))
         return jnp.concatenate(parts, axis=1)
 
@@ -149,48 +164,41 @@
         return pl.ds(pl.multiple_of(peer * message, message), message)
 
     def exchange(source, target, send, recv, kind):
-        def remote(peer):
+        def remote(peer, to):
             return pltpu.make_async_remote_copy(
                 src_ref=source.at[kind, span_of(peer), :], dst_ref=target.at[kind, span_of(me), :],
                 send_sem=send.at[kind, peer], recv_sem=recv.at[kind, me],
-                device_id=where(peer), device_id_type=MESH)
-
-        def start(i, c):
-            @pl.when(i != me)
-            def _():
-                remote(i).start()
-
-            @pl.when(i == me)
-            def _():
-                pltpu.make_async_copy(
-                    source.at[kind, span_of(me), :], target.at[kind, span_of(me), :],
-                    recv.at[kind, me]).start()
-            return c
-
-        def start_all(k, c):
-            remote(peer_of(k)).start()
-            return c
+                device_id=to, device_id_type=MESH)
+
+        def keep():
+            pltpu.make_async_copy(
+                source.at[kind, span_of(me), :], target.at[kind, span_of(me), :],
+                recv.at[kind, me]).start()
+
+        def start(g):
+            for i in range(g * GROUP, (g + 1) * GROUP):
+                @pl.when(i != me)
+                def _():
+                    remote(i, (i // n_model, i % n_model)).start()
+
+                @pl.when(i == me)
+                def _():
+                    keep()
 
         def arrive(i, c):
             at = target.at[kind, span_of(i), :]
             pltpu.make_async_copy(at, at, recv.at[kind, i]).wait()
             return c
 
-        def sent(k, c):
-            remote(peer_of(k)).wait_send()
-            return c
-
         def begin():
-            lax.fori_loop(1, n, start_all, 0)
-            pltpu.make_async_copy(
-                source.at[kind, span_of(me), :], target.at[kind, span_of(me), :],
-                recv.at[kind, me]).start()
+            others(lambda peer, to: remote(peer, to).start())
+            keep()
 
         return (
-            lambda g: lax.fori_loop(g * GROUP, (g + 1) * GROUP, start, 0),
+            start,
             begin,
             lambda g: lax.fori_loop(g * GROUP, (g + 1) * GROUP, arrive, 0),
-            lambda: lax.fori_loop(1, n, sent, 0),
+            lambda: others(lambda peer, to: remote(peer, to).wait_send()),
         )
 
     row_moves = [exchange(msg_out, msg_in, row_send, row_recv, kind) for kind in range(2)]
@@ -218,9 +226,9 @@
     r = iota((big, big), 0)
     c = iota((big, big), 1)
     unpack = ones_where(
-        (lax.div(r, seats) == lax.rem(c, per_row)) & (lax.rem(r, seats) == lax.div(c, per_row)))
+        (div(r, seats) == rem(c, per_row)) & (rem(r, seats) == div(c, per_row)))
     pack = ones_where(
-        (lax.div(c, seats) == lax.rem(r, per_row)) & (lax.rem(c, seats) == lax.div(r, per_row)))
+        (div(c, seats) == rem(r, per_row)) & (rem(c, seats) == div(r, per_row)))
 
     def fetch(kind, target, base):
         for g in range(groups):
@@ -329,11 +337,7 @@
             target[:, c0 * chunk:(c0 + 1) * chunk] = dot(
                 sel_t[c0 * rows:(c0 + 1) * rows, :], ret_in[kind])
 
-    def ask_sent(k, c):
-        ask_copy(peer_of(k)).wait_send()
-        return c
-
-    lax.fori_loop(1, n, ask_sent, 0)
+    others(lambda peer, to: ask_copy(peer, to).wait_send())
     for kind in range(2):
         row_moves[kind][3]()
         ret_moves[kind][3]()
@@ -401,7 +405,7 @@
             dma((n_model,)), dma((n_model,)), dma((n_model,)), dma((n_model,)),
         ],
         compiler_params=pltpu.CompilerParams(
-            collective_id=0, has_side_effects=True, vmem_limit_bytes=taken + ends + SPARE),
+            collective_id=0, has_side_effects=True, vmem_limit_bytes=max(taken + ends + SPARE, GRANT)),
         cost_estimate=pl.CostEstimate(
             flops=flops, bytes_accessed=4 * n_tok * width, transcendentals=2 * n_tok * slots),
     )(tokens, out_grad, down_rows, up_rows, wanted, chosen, gates)

time: 64.3 us -> 55.3 us (0.86)
  local copies, waits for them, and re-layouts: 14.1 us -> 7.38 us
  Pallas kernels: 49.2 us -> 47 us
    unnamed x17 -> x13, local copies, waits for them, and re-layouts: 14.1 us -> 7.38 us
    pallas_call x1, Pallas kernels: 49.2 us -> 47 us  [shards(): pl.pallas_call(functools.partial(kernel, n, n_model), out_shape=(jax.Shap...]
where the time goes in v4:
time: 55.3 us; the launch traced here: 55 us
  Pallas kernels  47 us (85%)
  local copies, waits for them, and re-layouts  7.38 us (13%)
  between operations  0.65 us (1%)
    pallas_call x1, Pallas kernels, shards(): pl.pallas_call(functools.partial(kernel, n, n_model), out_shape=(jax.Shap...  47 us
    unnamed x13, local copies, waits for them, and re-layouts  7.38 us

profile of v4, /device:TPU:0, one launch (start us, length us, event | category | flops | bytes accessed | tf_op | source)
XLA Modules:
  0.0 55.0 jit_solution(6919881792166740667)
XLA Ops:
  0.6 0.0 copy-start
  0.6 0.9 %copy-done = bf16[64,2048]{1,0:T(8,128)(2,1)S(1)} copy-done((bf16[64,2048]{1,0:T(8,128)(2,1)S(1)}, bf16[64,2048]{1,0:T(8,128)(2,1)}, u32[]{:S(2)}) %copy-start) | copy-done | bytes 262168
  1.6 0.0 copy-start.1
  1.6 0.9 %copy-done.1 = bf16[64,2048]{1,0:T(8,128)(2,1)S(1)} copy-done((bf16[64,2048]{1,0:T(8,128)(2,1)S(1)}, bf16[64,2048]{1,0:T(8,128)(2,1)}, u32[]{:S(2)}) %copy-start.1) | copy-done | bytes 262168
  2.5 0.0 copy-start.2
  2.5 0.9 %copy-done.2 = s32[2,2048,16]{1,2,0:T(8,128)S(1)} copy-done((s32[2,2048,16]{1,2,0:T(8,128)S(1)}, s32[2,2048,16]{1,2,0:T(8,128)}, u32[]{:S(2)}) %copy-start.2) | copy-done | bytes 262168
  3.5 0.0 copy-start.3
  3.5 0.9 %copy-done.3 = f32[2,2048,16]{1,2,0:T(8,128)S(1)} copy-done((f32[2,2048,16]{1,2,0:T(8,128)S(1)}, f32[2,2048,16]{1,2,0:T(8,128)}, u32[]{:S(2)}) %copy-start.3) | copy-done | bytes 262168
  4.4 0.0 copy-start.4
  4.4 0.7 %copy-done.4 = s32[1,32,2]{1,2,0:T(2,128)S(1)} copy-done((s32[1,32,2]{1,2,0:T(2,128)S(1)}, s32[1,32,2]{1,2,0:T(2,128)}, u32[]{:S(2)}) %copy-start.4) | copy-done | bytes 280
  5.1 47.0 %shard_map.94 = (bf16[512,2048]{1,0:T(8,128)(2,1)S(1)}, f32[64,2048]{1,0:T(8,128)S(1)}, f32[64,2048]{1,0:T(8,128)S(1)}) custom-call(bf16[2048,2048]{1,0:T(8,128)(2,1)} %tokens.1, bf16[2048,2048]{1,0:T(8,128)(2,1)} %grads.1, bf16[64,2048]{1,0:T(8,128)(2,1)S(1)} %copy-done, bf16[64,2048]{1,0:T(8,128)(2,1)S(1)} %copy-done.1, s32[2,32]{1,0:T(2,128)S(1)} %bitcast.11, ...), custom_call_target="tpu_custom_call" | custom-call | flops 2684354560 | bytes 16777216 | tf_op jit(solution)/shard_map/pallas_call | solution.py:393
  52.1 1.3 %copy.13 = bf16[512,2048]{1,0:T(8,128)(2,1)} copy(bf16[512,2048]{1,0:T(8,128)(2,1)S(1)} %get-tuple-element.6) | data formatting | bytes 4194304
  53.4 0.8 %copy.14 = f32[64,2048]{1,0:T(8,128)} copy(f32[64,2048]{1,0:T(8,128)S(1)} %get-tuple-element.7) | data formatting | bytes 1048576
  54.2 0.8 %copy.15 = f32[64,2048]{1,0:T(8,128)} copy(f32[64,2048]{1,0:T(8,128)S(1)} %get-tuple-element.8) | data formatting | bytes 1048576
Async XLA Ops:
  0.6 1.0 %copy-start = (bf16[64,2048]{1,0:T(8,128)(2,1)S(1)}, bf16[64,2048]{1,0:T(8,128)(2,1)}, u32[]{:S(2)}) copy-start(bf16[64,2048]{1,0:T(8,128)(2,1)} %down_rows.1) | copy-start | bytes 786436
  1.6 0.9 %copy-start.1 = (bf16[64,2048]{1,0:T(8,128)(2,1)S(1)}, bf16[64,2048]{1,0:T(8,128)(2,1)}, u32[]{:S(2)}) copy-start(bf16[64,2048]{1,0:T(8,128)(2,1)} %up_rows.1) | copy-start | bytes 786436
  2.5 0.9 %copy-start.2 = (s32[2,2048,16]{1,2,0:T(8,128)S(1)}, s32[2,2048,16]{1,2,0:T(8,128)}, u32[]{:S(2)}) copy-start(s32[2,2048,16]{1,2,0:T(8,128)} %param.12) | copy-start | bytes 786436
  3.5 0.9 %copy-start.3 = (f32[2,2048,16]{1,2,0:T(8,128)S(1)}, f32[2,2048,16]{1,2,0:T(8,128)}, u32[]{:S(2)}) copy-start(f32[2,2048,16]{1,2,0:T(8,128)} %param.13) | copy-start | bytes 786436
  4.4 0.7 %copy-start.4 = (s32[1,32,2]{1,2,0:T(2,128)S(1)}, s32[1,32,2]{1,2,0:T(2,128)}, u32[]{:S(2)}) copy-start(s32[1,32,2]{1,2,0:T(2,128)} %param.11) | copy-start | bytes 772
